TPU v7x, 512 devices: a whole 4x8x8 slice. The times are simulated.
512 devices in a mesh: rec: 16 (over z, core), frame: 32 (over x, y).
Axes of the slice: x: 4, y: 8, z: 8, core: 2. Of those that a mesh axis runs over, the one named last changes fastest.
Arguments:
- frames: bfloat16 [16, 49152, 256], P('rec', 'frame'), may hold values from -10 to 10
- texts: bfloat16 [32, 224, 256], P('rec', 'frame'), may hold values from -100 to 100
- pair_rec: int32 [32, 1], replicated, may hold values from 0 to 15, as said below
- pair_text: int32 [32], replicated, may hold values from 0 to 31, as said below
- pair_label: int32 [32], replicated, may hold values 0 or 1
Outputs:
- loss: float32 [], replicated
- grad_frames: bfloat16 [16, 49152, 256], P('rec', 'frame')
- grad_texts: bfloat16 [32, 224, 256], P('rec', 'frame')
Inputs may be any that keep to these rules, and one draw needn't show every extreme that they name: `pair_rec`: no recording is named by more than 6 pairs, some recording by exactly 6, and every recording by at least one. A pair's text is held by the index of rec one after, one before, or 8 after its recording (counted round): pair_text // 2 = (pair_rec + k) mod 16 with k one of 1, 15, 8.
All inputs are finite; a program needn't handle non-finite values.
Results may differ from a plain program's by a relative error of at most 0.0085.
Values may be sent and summed in bfloat16 or wider, within the bound.
A program may use at most 64 MiB of HBM per device.

v0:
```python
import jax
import jax.numpy as jnp
from jax import lax
from jax.sharding import PartitionSpec as P

MOST = 6
EPS = 1e-06
TEMP = 10.0
BIAS = -1.0
LOSS_SCALE = 2048.0


def slot_tables(pair_rec, pair_text, pair_label, here, most):
    record = pair_rec[:, 0]
    count = record.shape[0]
    order = jnp.arange(count, dtype=jnp.int32)
    same = (record[:, None] == record[None, :]).astype(jnp.int32)
    earlier = (order[None, :] < order[:, None]).astype(jnp.int32)
    rank = jnp.sum(same * earlier, axis=1)
    places = jnp.arange(most, dtype=jnp.int32)
    chosen = ((record[None, :] == here) & (rank[None, :] == places[:, None])).astype(jnp.int32)
    valid = jnp.sum(chosen, axis=1)
    slot_text = jnp.sum(chosen * pair_text[None, :], axis=1)
    sign = jnp.sum(chosen * (2 * pair_label[None, :] - 1), axis=1)
    return (valid, slot_text, sign)


def pair_terms(score, valid, sign, tokens):
    margin = -sign * (TEMP * score + BIAS)
    loss_part = valid * jax.nn.softplus(margin)
    grad_cos = -LOSS_SCALE * TEMP * valid * sign * jax.nn.sigmoid(margin) / tokens
    return (loss_part, grad_cos)


def body(frames, texts, pair_rec, pair_text, pair_label):
    here = lax.axis_index("rec")
    part = lax.axis_index("frame")
    owned, width_rows, width = texts.shape
    tokens = width_rows * lax.axis_size("frame")
    n_text = owned * lax.axis_size("rec")
    valid, slot_text, sign = slot_tables(pair_rec, pair_text, pair_label, here, MOST)
    valid_f = valid.astype(jnp.float32)
    sign_f = sign.astype(jnp.float32)
    picks = (
        (slot_text[:, None] == jnp.arange(n_text, dtype=jnp.int32)[None, :]) & (valid[:, None] > 0)
    ).astype(jnp.bfloat16)
    whole = lax.all_gather(texts, "frame", axis=1, tiled=True)
    query_vectors = jnp.einsum(
        "jc,cgx->jgx",
        picks,
        lax.all_gather(whole, "rec", axis=0, tiled=True),
        preferred_element_type=jnp.float32,
    ).astype(jnp.bfloat16)
    upstream_signal = frames[0]
    logit_scale = width ** (-0.5)
    pair_scores = (
        jnp.einsum(
            "ype,je->ypj", query_vectors, upstream_signal, preferred_element_type=jnp.float32
        )
        * logit_scale
    )
    local_max = jnp.max(pair_scores, axis=2)
    row_max = lax.pmax(local_max, "frame")
    expo = jnp.exp(pair_scores - row_max[..., None])
    batch_weights = expo.astype(jnp.bfloat16)
    value_partial = jnp.einsum(
        "pqx,xh->pqh", batch_weights, upstream_signal, preferred_element_type=jnp.float32
    )
    query_f = query_vectors.astype(jnp.float32)
    q_norm = lax.rsqrt(jnp.sum(query_f * query_f, axis=2) + EPS)
    q_unit = query_f * q_norm[..., None]
    context = lax.psum(value_partial, "frame")
    c_norm = lax.rsqrt(jnp.sum(context * context, axis=2) + EPS)
    c_unit = context * c_norm[..., None]
    cos = jnp.sum(q_unit * c_unit, axis=2)
    score = jnp.mean(cos, axis=1)
    loss_part, grad_cos = pair_terms(score, valid_f, sign_f, tokens)
    weight = grad_cos[:, None, None]
    d_context = weight * (q_unit - cos[..., None] * c_unit) * c_norm[..., None]
    direct = weight * (c_unit - cos[..., None] * q_unit) * q_norm[..., None]
    direct_own = lax.dynamic_slice_in_dim(direct, part * width_rows, width_rows, 1)
    context_batch_gradient = d_context.astype(jnp.bfloat16)
    weight_gradient = jnp.einsum(
        "ype,je->ypj", context_batch_gradient, upstream_signal, preferred_element_type=jnp.float32
    )
    score_gradient = (expo * weight_gradient * logit_scale).astype(jnp.bfloat16)
    d_query = lax.psum_scatter(
        jnp.einsum(
            "slf,fd->lsd", score_gradient, upstream_signal, preferred_element_type=jnp.float32
        ),
        "frame",
        scatter_dimension=0,
        tiled=True,
    )
    d_query = d_query + jnp.transpose(direct_own, (1, 0, 2))
    text_term = jnp.einsum(
        "st,lsd->tld", picks.astype(jnp.float32), d_query, precision=lax.Precision.HIGHEST
    )
    grad_texts = lax.psum_scatter(text_term, "rec", scatter_dimension=0, tiled=True).astype(
        jnp.bfloat16
    )
    frame_loss_piece = jnp.einsum(
        "cvm,cvz->mz", score_gradient, query_vectors, preferred_element_type=jnp.float32
    )
    frame_loss_piece = frame_loss_piece + jnp.einsum(
        "cvm,cvz->mz", batch_weights, context_batch_gradient, preferred_element_type=jnp.float32
    )
    grad_frames = frame_loss_piece.astype(jnp.bfloat16)[None]
    loss = lax.psum(jnp.sum(loss_part), "rec")
    return (loss, grad_frames, grad_texts)


def solution(mesh):
    return jax.shard_map(
        body,
        mesh=mesh,
        in_specs=(P("rec", "frame", None), P("rec", "frame", None), P(), P(), P()),
        out_specs=(P(), P("rec", "frame", None), P("rec", "frame", None)),
        check_vma=False,
    )
```

profile of v0, /device:TPU:16, one launch (start us, length us, event | category | flops | bytes accessed | tf_op | source)
XLA Modules:
  0.0 644.4 jit_solution(15901261809968272552)
XLA Ops:
  7.2 0.0 copy-start
  7.2 0.0 all-gather.2.cloned.1.call-start
  7.2 49.8 %all_gather.6 = bf16[2,224,256]{2,0,1:T(2,128)(2,1)S(1)} all-gather(bf16[2,7,256]{2,0,1:T(2,128)(2,1)} %param.6), channel_id=1, replica_groups=mesh['rec'=16,'frame'=32] {'frame'}, dimensions={1}, use_global_device_ids=true | all-gather | bytes 236544 | tf_op jit(solution)/shard_map/all_gather | solution.py:47
  57.0 0.7 copy.20
  57.7 0.0 all-gather.2.cloned.1.call-update
  57.8 0.0 all-reduce.5.cloned.1.call-start
  57.8 0.9 select_reduce_fusion
  58.7 0.7 broadcast_compare_fusion.1
  59.4 0.7 multiply_add_fusion
  60.1 1.3 select_reduce_fusion.2
  61.4 0.0 copy-start.8
  61.4 43.4 %all-gather.2.cloned.1.call-done = bf16[32,224,256]{2,1,0:T(8,128)(2,1)} async-done(((bf16[2,224,256]{2,1,0:T(8,128)(2,1)}), bf16[32,224,256]{2,1,0:T(8,128)(2,1)}) %all-gather.2.cloned.1.call-update) | async-done | bytes 3670032 | tf_op jit(solution)/shard_map/all_gather | solution.py:51
  104.7 0.0 copy-done.9
  104.7 4.3 fusion.6
  109.0 0.0 copy-done.4
  109.0 0.0 copy-done.8
  109.0 0.0 copy-done
  109.0 4.4 multiply_reduce_fusion
  113.4 71.4 %pmax.7 = f32[6,224]{1,0:T(8,128)S(1)} all-reduce(f32[6,224]{1,0:T(8,128)S(1)} %get-tuple-element.17), channel_id=1, replica_groups=mesh['rec'=16,'frame'=32] {'frame'}, use_global_device_ids=true, to_apply=%region_6.0 | all-reduce | flops 1344 | bytes 10752 | tf_op jit(solution)/shard_map/pmax | solution.py:63
  184.8 4.9 fusion.13
  189.7 2.1 copy.23
  191.7 0.0 all-reduce.5.cloned.1.call-update
  191.8 0.2 reduce-scatter.3.cloned.1.call-start
  192.0 0.7 add_rsqrt_fusion.1
  192.6 157.1 %all-reduce.5.cloned.1.call-done = f32[6,224,256]{2,0,1:T(8,128)} async-done(((f32[6,224,256]{2,0,1:T(8,128)}), f32[6,224,256]{2,0,1:T(8,128)}) %all-reduce.5.cloned.1.call-update) | async-done | bytes 1376272 | tf_op jit(solution)/shard_map/psum | solution.py:72
  349.7 1.9 multiply_reduce_fusion.1
  351.6 2.4 multiply_reduce_fusion.2
  354.0 1.4 fusion.44
  355.4 0.0 copy-done.1
  355.4 1.8 convert_multiply_fusion
  357.2 4.9 multiply_convert_fusion
  362.2 1.3 fusion.10
  363.5 0.7 copy-done.10
  364.2 2.1 copy.47
  366.2 0.0 reduce-scatter.3.cloned.1.call-update
  366.2 1.3 dynamic-slice
  368.2 0.7 constant_dynamic-slice_fusion
  368.9 0.7 constant_dynamic-slice_fusion.1
  369.6 5.7 convolution_bitcast_fusion
  375.2 0.0 copy-done.11
  375.3 0.0 copy-start.5
  375.3 0.0 copy-start.7
  375.3 2.3 fusion.5
  377.6 209.2 %reduce-scatter.3.cloned.1.call-done = f32[7,6,256]{2,1,0:T(8,128)} async-done(((f32[224,6,256]{2,1,0:T(8,128)}), f32[7,6,256]{2,1,0:T(8,128)}) %reduce-scatter.3.cloned.1.call-update) | async-done | bytes 43024 | tf_op jit(solution)/shard_map/reduce_scatter | solution.py:87
  586.9 0.0 copy-done.7
  586.9 1.3 fusion.27
  588.2 49.1 %all-reduce.6 = (f32[]{:T(128)}, bf16[32,7,256]{2,0,1:T(8,128)(2,1)S(1)}) all-reduce(f32[]{:T(128)} %get-tuple-element.14, f32[32,7,256]{2,0,1:T(8,128)S(1)} %fusion.27), channel_id=1, replica_groups=mesh['rec'=16,'frame'=32] {'rec'}, use_global_device_ids=true, to_apply=%region_11.12 | all-reduce | flops 57345 | bytes 344072 | tf_op jit(solution)/shard_map/psum | solution.py:109
  637.3 0.6 dynamic-slice_convert_fusion
  (14 shorter events, 0.1 us)
Async XLA Ops:
  7.2 101.8 %copy-start = (bf16[1,1536,256]{2,1,0:T(8,128)(2,1)S(1)}, bf16[1,1536,256]{2,1,0:T(8,128)(2,1)}, u32[]{:S(2)}) copy-start(bf16[1,1536,256]{2,1,0:T(8,128)(2,1)} %param.5) | copy-start | bytes 2359300
  7.2 97.5 %all-gather.2.cloned.1.call-start = ((), (), s32[]{:S(2)}) async-start(), calls=%async_computation.1 | async-start | bytes 3899392 | tf_op jit(solution)/shard_map/all_gather | solution.py:51
  57.8 291.9 %all-reduce.5.cloned.1.call-start = ((), (), s32[]{:S(2)}) async-start(), calls=%async_computation.2 | async-start | bytes 3670016 | tf_op jit(solution)/shard_map/psum | solution.py:72
  61.3 43.4 %copy-start.9 = (s32[6]{0:T(128)}, s32[6]{0:T(128)S(1)}, u32[]{:S(2)}) copy-start(s32[6]{0:T(128)S(1)} %get-tuple-element.7) | copy-start | bytes 76
  61.3 47.6 %copy-start.4 = (s32[6]{0:T(128)}, s32[6]{0:T(128)S(1)}, u32[]{:S(2)}) copy-start(s32[6]{0:T(128)S(1)} %get-tuple-element.6) | copy-start | bytes 76
  61.4 47.6 %copy-start.8 = (pred[6]{0:T(512)(128)(4,1)}, pred[6]{0:T(512)(128)(4,1)S(1)}, u32[]{:S(2)}) copy-start(pred[6]{0:T(512)(128)(4,1)S(1)} %broadcast_compare_fusion) | copy-start | bytes 22
  191.8 395.1 %reduce-scatter.3.cloned.1.call-start = ((), (), s32[]{:S(2)}) async-start(), calls=%async_computation.3 | async-start | bytes 1892352 | tf_op jit(solution)/shard_map/reduce_scatter | solution.py:87
  349.7 5.7 copy-start.1
  354.0 3.2 copy-start.3
  355.4 6.8 %copy-start.6 = (f32[6]{0:T(128)}, f32[6]{0:T(128)S(1)}, u32[]{:S(2)}) copy-start(f32[6]{0:T(128)S(1)} %get-tuple-element.13) | copy-start | bytes 76
  357.2 5.0 copy-start.2
  362.2 2.0 copy-start.10
  369.6 5.7 copy-start.11
  375.3 211.6 %copy-start.5 = (s32[6]{0:T(128)S(1)}, s32[6]{0:T(128)}, u32[]{:S(2)}) copy-start(s32[6]{0:T(128)} %copy-done.4) | copy-start | bytes 76
  375.3 211.6 %copy-start.7 = (f32[6]{0:T(128)S(1)}, f32[6]{0:T(128)}, u32[]{:S(2)}) copy-start(f32[6]{0:T(128)} %copy-done.6) | copy-start | bytes 76
Sparse Core Ops, SparseCore 0:
  57.9 46.7 all-gather.1
  191.9 157.7 all-reduce.4
  366.4 220.4 reduce-scatter.2
where the time goes:
time: 645 us; the launch traced here: 644 us
  waiting for transfers between devices  410 us (64%)
  blocking collectives  170 us (26%)
  matrix products  29 us (4%)
  between operations  14.6 us (2%)
  other arithmetic  11.7 us (2%)
  local copies, waits for them, and re-layouts  8.88 us (1%)
    reduce_scatter x1, waiting for transfers between devices, body(): lax.psum_scatter(jnp.einsum('slf,fd->lsd', score_gradient, upstream_signa...  209 us
    psum x1, waiting for transfers between devices, body(): context = lax.psum(value_partial, 'frame')  157 us
    pmax x1, blocking collectives, body(): row_max = lax.pmax(local_max, 'frame')  71.4 us
    all_gather x1, blocking collectives, body(): whole = lax.all_gather(texts, 'frame', axis=1, tiled=True)  49.8 us
    psum x1, blocking collectives, body(): loss = lax.psum(jnp.sum(loss_part), 'rec')  49.1 us
    all_gather x1, waiting for transfers between devices, body(): lax.all_gather(whole, 'rec', axis=0, tiled=True)  43.4 us
  transfers between devices with their start and end apart: 3, of which 3 were waited for; matrix products, arithmetic and copies ran while one was open for 2% of the time, Pallas kernels for 0%

commit v1 on v0

--- a/solution.py
+++ b/solution.py
@@ -48,7 +48,9 @@
     query_vectors = jnp.einsum(
         "jc,cgx->jgx",
         picks,
-        lax.all_gather(whole, "rec", axis=0, tiled=True),
+        jnp.concatenate(
+            lax.all_to_all(jnp.stack([whole] * lax.axis_size("rec")), "rec", 0, 0), axis=0
+        ),
         preferred_element_type=jnp.float32,
     ).astype(jnp.bfloat16)
     upstream_signal = frames[0]

time: 645 us -> 708 us (1.098)
  waiting for transfers between devices: 410 us -> 448 us
  local copies, waits for them, and re-layouts: 8.88 us -> 28 us
  starting transfers between devices: 0.3 us -> 10.9 us
    all_to_all x0 -> x1, waiting for transfers between devices: none -> 81.7 us  [body(): lax.all_to_all(jnp.stack([whole] * lax.axis_size('rec')), 'rec', 0, 0)]
    all_gather x1 -> x0, waiting for transfers between devices: 43.4 us -> none  [body(): lax.all_gather(whole, 'rec', axis=0, tiled=True)]
    all_to_all x0 -> x1, starting transfers between devices: none -> 10.6 us  [body(): lax.all_to_all(jnp.stack([whole] * lax.axis_size('rec')), 'rec', 0, 0)]
    all_to_all x0 -> x1, local copies, waits for them, and re-layouts: none -> 8.06 us  [body(): lax.all_to_all(jnp.stack([whole] * lax.axis_size('rec')), 'rec', 0, 0)]
where the time goes in v1:
time: 708 us; the launch traced here: 707 us
  waiting for transfers between devices  448 us (63%)
  blocking collectives  168 us (24%)
  local copies, waits for them, and re-layouts  28 us (4%)
  matrix products  27.6 us (4%)
  between operations  14.9 us (2%)
  starting transfers between devices  10.9 us (2%)
  other arithmetic  8.97 us (1%)
    reduce_scatter x1, waiting for transfers between devices, body(): lax.psum_scatter(jnp.einsum('slf,fd->lsd', score_gradient, upstream_signa...  209 us
    psum x1, waiting for transfers between devices, body(): context = lax.psum(value_partial, 'frame')  158 us
    all_to_all x1, waiting for transfers between devices, body(): lax.all_to_all(jnp.stack([whole] * lax.axis_size('rec')), 'rec', 0, 0)  81.7 us
    pmax x1, blocking collectives, body(): row_max = lax.pmax(local_max, 'frame')  69.3 us
    all_gather x1, blocking collectives, body(): whole = lax.all_gather(texts, 'frame', axis=1, tiled=True)  49.8 us
    psum x1, blocking collectives, body(): loss = lax.psum(jnp.sum(loss_part), 'rec')  49.1 us
  transfers between devices with their start and end apart: 3, of which 3 were waited for; matrix products, arithmetic and copies ran while one was open for 2% of the time, Pallas kernels for 0%

profile of v1, /device:TPU:16, one launch (start us, length us, event | category | flops | bytes accessed | tf_op | source)
XLA Modules:
  0.0 706.9 jit_solution(3332339999999266186)
XLA Ops:
  7.2 0.0 copy-start
  7.2 49.8 %all_gather.3 = bf16[2,224,256]{2,0,1:T(2,128)(2,1)S(1)} all-gather(bf16[2,7,256]{2,0,1:T(2,128)(2,1)} %param.6), channel_id=1, replica_groups=mesh['rec'=16,'frame'=32] {'frame'}, dimensions={1}, use_global_device_ids=true | all-gather | bytes 236544 | tf_op jit(solution)/shard_map/all_gather | solution.py:47
  57.0 4.7 stack.2
  61.7 10.6 %all-to-all-start = ((bf16[16,2,224,256]{3,1,2,0:T(2,128)(2,1)}), bf16[16,2,224,256]{3,1,2,0:T(2,128)(2,1)}, u32[]{:S(2)}, u32[]{:S(2)}) async-start(bf16[16,2,224,256]{3,1,2,0:T(2,128)(2,1)} %stack.2), calls=%async_computation | async-start | bytes 7340032 | tf_op jit(solution)/shard_map/all_to_all | solution.py:52
  72.3 0.0 all-reduce.5.cloned.1.call-start
  72.3 0.0 copy-done.11
  72.3 0.2 select_reduce_fusion
  72.5 0.0 copy-done.12
  72.5 0.0 copy-done.10
  72.5 0.6 select_reduce_fusion.2
  73.2 0.5 copy-done.9
  73.7 81.7 %all-to-all-done = bf16[16,2,224,256]{3,1,2,0:T(2,128)(2,1)} async-done(((bf16[16,2,224,256]{3,1,2,0:T(2,128)(2,1)}), bf16[16,2,224,256]{3,1,2,0:T(2,128)(2,1)}, u32[]{:S(2)}, u32[]{:S(2)}) %all-to-all-start) | async-done | bytes 3670048 | tf_op jit(solution)/shard_map/all_to_all | solution.py:52
  155.4 8.1 %copy.19 = bf16[16,2,224,256]{3,1,0,2:T(2,128)(2,1)} copy(bf16[16,2,224,256]{3,1,2,0:T(2,128)(2,1)} %all-to-all-done) | data formatting | bytes 7340032 | tf_op jit(solution)/shard_map/all_to_all | solution.py:52
  163.4 6.6 reshape.59
  170.0 0.0 copy-done.8
  170.0 2.8 fusion.4
  172.8 4.4 multiply_reduce_fusion
  177.2 69.3 %pmax.7 = f32[6,224]{1,0:T(8,128)S(1)} all-reduce(f32[6,224]{1,0:T(8,128)S(1)} %get-tuple-element.17), channel_id=1, replica_groups=mesh['rec'=16,'frame'=32] {'frame'}, use_global_device_ids=true, to_apply=%region_6.0 | all-reduce | flops 1344 | bytes 10752 | tf_op jit(solution)/shard_map/pmax | solution.py:65
  246.6 4.9 fusion.8
  251.4 2.1 copy.21
  253.5 0.0 all-reduce.5.cloned.1.call-update
  253.5 0.2 reduce-scatter.3.cloned.1.call-start
  253.7 0.7 add_rsqrt_fusion.1
  254.4 157.5 %all-reduce.5.cloned.1.call-done = f32[6,224,256]{2,0,1:T(8,128)} async-done(((f32[6,224,256]{2,0,1:T(8,128)}), f32[6,224,256]{2,0,1:T(8,128)}) %all-reduce.5.cloned.1.call-update) | async-done | bytes 1376272 | tf_op jit(solution)/shard_map/psum | solution.py:74
  412.0 1.9 multiply_reduce_fusion.1
  413.8 2.4 multiply_reduce_fusion.2
  416.3 1.4 fusion.39
  417.7 1.8 convert_multiply_fusion
  419.5 4.9 multiply_convert_fusion
  424.4 0.0 copy-done.6
  424.4 0.0 copy-done.2
  424.4 0.0 copy-start.13
  424.4 1.3 fusion.5
  425.7 0.7 copy-done.13
  426.4 2.1 copy.39
  428.5 0.0 reduce-scatter.3.cloned.1.call-update
  428.5 1.3 dynamic-slice
  430.4 0.7 constant_dynamic-slice_fusion
  431.1 0.7 constant_dynamic-slice_fusion.1
  431.8 5.7 convolution_bitcast_fusion
  437.5 0.0 copy-done.14
  437.5 0.0 copy-start.5
  437.5 0.0 copy-start.7
  437.5 2.3 fusion.3
  439.9 209.2 %reduce-scatter.3.cloned.1.call-done = f32[7,6,256]{2,1,0:T(8,128)} async-done(((f32[224,6,256]{2,1,0:T(8,128)}), f32[7,6,256]{2,1,0:T(8,128)}) %reduce-scatter.3.cloned.1.call-update) | async-done | bytes 43024 | tf_op jit(solution)/shard_map/reduce_scatter | solution.py:89
  649.1 1.3 fusion.22
  650.4 49.1 %all-reduce.6 = (f32[]{:T(128)}, bf16[32,7,256]{2,0,1:T(8,128)(2,1)S(1)}) all-reduce(f32[]{:T(128)} %get-tuple-element.14, f32[32,7,256]{2,0,1:T(8,128)S(1)} %fusion.22), channel_id=1, replica_groups=mesh['rec'=16,'frame'=32] {'rec'}, use_global_device_ids=true, to_apply=%region_11.12 | all-reduce | flops 57345 | bytes 344072 | tf_op jit(solution)/shard_map/psum | solution.py:111
  699.5 0.6 dynamic-slice_convert_fusion
  (21 shorter events, 0.1 us)
Async XLA Ops:
  7.2 165.6 %copy-start = (bf16[1,1536,256]{2,1,0:T(8,128)(2,1)S(1)}, bf16[1,1536,256]{2,1,0:T(8,128)(2,1)}, u32[]{:S(2)}) copy-start(bf16[1,1536,256]{2,1,0:T(8,128)(2,1)} %param.5) | copy-start | bytes 2359300
  61.7 10.7 %copy-start.11 = (s32[32,1]{0,1:T(1,128)S(1)}, s32[32,1]{0,1:T(1,128)}, u32[]{:S(2)}) copy-start(s32[32,1]{0,1:T(1,128)} %param.7) | copy-start | bytes 388
  61.7 10.9 %copy-start.12 = (s32[32]{0:T(128)S(1)}, s32[32]{0:T(128)}, u32[]{:S(2)}) copy-start(s32[32]{0:T(128)} %param.9) | copy-start | bytes 388
  61.7 10.9 %copy-start.10 = (s32[32]{0:T(128)S(1)}, s32[32]{0:T(128)}, u32[]{:S(2)}) copy-start(s32[32]{0:T(128)} %param.8) | copy-start | bytes 388
  61.7 93.7 %all-to-all-start = ((bf16[16,2,224,256]{3,1,2,0:T(2,128)(2,1)}), bf16[16,2,224,256]{3,1,2,0:T(2,128)(2,1)}, u32[]{:S(2)}, u32[]{:S(2)}) async-start(bf16[16,2,224,256]{3,1,2,0:T(2,128)(2,1)} %stack.2), calls=%async_computation | async-start | bytes 7340032 | tf_op jit(solution)/shard_map/all_to_all | solution.py:52
  72.3 339.7 %all-reduce.5.cloned.1.call-start = ((), (), s32[]{:S(2)}) async-start(), calls=%async_computation.2 | async-start | bytes 3670016 | tf_op jit(solution)/shard_map/psum | solution.py:74
  73.2 0.5 copy-start.9
  73.2 96.8 %copy-start.4 = (s32[6]{0:T(128)}, s32[6]{0:T(128)S(1)}, u32[]{:S(2)}) copy-start(s32[6]{0:T(128)S(1)} %get-tuple-element.6) | copy-start | bytes 76
  73.7 96.3 %copy-start.8 = (pred[6]{0:T(512)(128)(4,1)}, pred[6]{0:T(512)(128)(4,1)S(1)}, u32[]{:S(2)}) copy-start(pred[6]{0:T(512)(128)(4,1)S(1)} %broadcast_compare_fusion) | copy-start | bytes 22
  253.5 395.6 %reduce-scatter.3.cloned.1.call-start = ((), (), s32[]{:S(2)}) async-start(), calls=%async_computation.3 | async-start | bytes 1892352 | tf_op jit(solution)/shard_map/reduce_scatter | solution.py:89
  412.0 5.7 copy-start.1
  416.3 3.2 copy-start.3
  417.6 6.8 copy-start.6
  419.5 5.0 copy-start.2
  424.4 2.0 copy-start.13
  431.8 5.7 copy-start.14
  437.5 211.6 %copy-start.5 = (s32[6]{0:T(128)S(1)}, s32[6]{0:T(128)}, u32[]{:S(2)}) copy-start(s32[6]{0:T(128)} %copy-done.4) | copy-start | bytes 76
  437.5 211.6 %copy-start.7 = (f32[6]{0:T(128)S(1)}, f32[6]{0:T(128)}, u32[]{:S(2)}) copy-start(f32[6]{0:T(128)} %copy-done.6) | copy-start | bytes 76
Sparse Core Ops, SparseCore 0:
  253.6 158.2 all-reduce.4
  428.6 220.4 reduce-scatter.2
